TPU v7x, 32 devices: a whole 2x2x4 slice. The times are simulated.
32 devices in a mesh: rep: 2 (over y), pool: 16 (over z, x, core).
Axes of the slice: x: 2, y: 2, z: 4, core: 2. Of those that a mesh axis runs over, the one named last changes fastest.
Arguments:
- pool_kv: bfloat16 [128, 8, 16, 256], P(('rep', 'pool')), parts along dimension 0, may hold values from -6 to 6
- prefix_table: int32 [4, 32], P('rep'), parts along dimension 0, may hold values from 0 to 63, as said below
- prefix_count: int32 [4], P('rep'), parts along dimension 0, may hold values from 17 to 32, as said below
- prefill_q: bfloat16 [32, 512, 1024], P(('rep', 'pool')), parts along dimension 0, may hold values from -25 to 25
- prefill_new_kv: bfloat16 [32, 512, 256], P(('rep', 'pool')), parts along dimension 0, may hold values from -6 to 6
- decode_q: bfloat16 [512, 8192], P(('rep', 'pool')), parts along dimension 0, may hold values from -25 to 25
- decode_new: bfloat16 [512, 2048], P(('rep', 'pool')), parts along dimension 0, may hold values from -6 to 6
- decode_cache: bfloat16 [32, 128, 2, 64, 256], P(('rep', 'pool')), parts along dimension 0, may hold values from -6 to 6
- decode_group: int32 [512, 1], P('rep'), parts along dimension 0, may hold values from 0 to 3; in each aligned block of 16 rows (0 to 15, 16 to 31, ...) at most 8 rows name the same one
- cached_len: int32 [512], P('rep'), parts along dimension 0, may hold values from 1 to 64, 8192 in all
Outputs:
- prefill_out: bfloat16 [32, 512, 1024], P(('rep', 'pool')), parts along dimension 0
- decode_out: bfloat16 [512, 8192], P(('rep', 'pool')), parts along dimension 0
There are 2 independent parts, one for each index of `rep`. A program takes and returns all parts, laid end to end along the dimension named above; each array names one. Nothing has to cross between parts.
Inputs may be any that keep to these rules, and one draw needn't show every extreme that they name: prefix_table[g, j] = o * 4 + b names block b of owner o. No block appears twice in the table. Among the first prefix_count[g] entries of a row, every owner holds at most 2; entries from prefix_count[g] on are not read. `prefix_count`: at least one request has 32 blocks. `decode_group`: among the rows of one home device, no group is named by more than 8 rows.
All inputs are finite; a program needn't handle non-finite values.
Results may differ from a plain program's by a relative error of at most 0.0055.
Values may be sent and summed in bfloat16 or wider, within the bound.
No kernel may reach another device: no remote copies, remote signals or barrier semaphores. Data moves between devices by JAX's collectives and lax.ppermute only.
A program may use at most 128 MiB of HBM per device.

v0:
```python
import functools

import jax
import jax.numpy as jnp
from jax import lax
from jax.experimental import pallas as pl
from jax.experimental.pallas import tpu as pltpu
from jax.sharding import PartitionSpec as P

PGRP = 8
DGRP = 4
PCAP = 2
PLANE = 4
LANES = 128
MASKED = -1e30
LOG2E = 1.4426950408889634


def any_spec():
    return pl.BlockSpec(memory_space=pl.ANY)


def smem_spec():
    return pl.BlockSpec(memory_space=pltpu.SMEM)


def in_hbm(x):
    return pltpu.with_memory_space_constraint(x, pltpu.HBM)


def vmem_spec():
    return pl.BlockSpec(memory_space=pltpu.VMEM)


def pack_kernel(head_rows, groups, table, count, q, pool, out, *rest):
    shares = rest[:PLANE]
    rows_scr, stage, group_fill, sems, block_sems = rest[PLANE:]
    flying = send_blocks(table, count, pool, shares, block_sems)
    decode_groups = out.shape[0]
    row_count = q.shape[0]
    head_total = q.shape[1] // LANES
    device = lax.axis_index("pool")
    for a in range(decode_groups):
        group_fill[a] = 0
    for h in range(head_total):
        rows_scr[pl.ds(h, row_count, stride=head_total), :] = q[
            :, h * LANES : (h + 1) * LANES
        ].astype(jnp.float32)
    homes = []
    for i in range(row_count):
        a = groups[device * row_count + i]
        c = group_fill[a]
        group_fill[a] = c + 1
        homes.append((a, c))
    copies = []
    for m in range(DGRP):
        for i, (a, c) in enumerate(homes):
            first = i * head_total + m * head_rows
            stage[m, a, pl.ds(pl.multiple_of(c * head_rows, 16), head_rows), :] = rows_scr[
                first : first + head_rows, :
            ].astype(out.dtype)
        copy = pltpu.make_async_copy(stage.at[m], out.at[:, m], sems.at[m])
        copy.start()
        copies.append(copy)
    for copy in copies + flying:
        copy.wait()


def send_blocks(table, count, pool, outs, sems):
    blocks_here = pool.shape[0]
    group_count, most_blocks = table.shape
    device = lax.axis_index("pool")
    first_block = device * blocks_here
    flying = []
    for g in range(group_count):

        def scan_table(j, carry):
            seen, chosen = carry
            entry = table[g, j]
            mine = (entry >= first_block) & (entry < first_block + blocks_here) & (j < count[g])
            chosen = tuple(
                jnp.where(mine & (seen == k), entry - first_block, chosen[k]) for k in range(PCAP)
            )
            return seen + mine.astype(jnp.int32), chosen

        start = (jnp.int32(0), tuple(jnp.int32(0) for _ in range(PCAP)))
        _, chosen = lax.fori_loop(0, most_blocks, scan_table, start, unroll=8)
        if g >= 2:
            for copy in flying.pop(0):
                copy.wait()
        copies = []
        for t in range(PLANE):
            for k in range(PCAP):
                copy = pltpu.make_async_copy(
                    pool.at[chosen[k], :, (device % PLANE) ^ t],
                    outs[t].at[:, g, k],
                    sems.at[((g % 2) * PLANE + t) * PCAP + k],
                )
                copy.start()
                copies.append(copy)
        flying.append(copies)
    return [copy for copies in flying for copy in copies]


def partner(plane, step, planes):
    return plane ^ step if planes & (planes - 1) == 0 else (plane + step) % planes


def regroup_kernel(planes, *rest):
    held, outs, sems = rest[:PLANE], rest[PLANE:-1], rest[-1]
    mine = lax.axis_index("pool") // PLANE
    per_group = PGRP // PLANE
    copies = []
    for step in range(planes):
        there = partner(mine, step, planes)
        for t in range(PLANE):
            copy = pltpu.make_async_copy(
                held[t].at[there % per_group, there // per_group],
                outs[step].at[t],
                sems.at[step * PLANE + t],
            )
            copy.start()
            copies.append(copy)
    for copy in copies:
        copy.wait()


def fetch_block(cache, listed, i, chunk, held, place, sem):
    return pltpu.make_async_copy(
        cache.at[pl.ds(listed[1 + i] * chunk, chunk)], held.at[pl.ds(place * chunk, chunk)], sem
    )


def plan_kernel(
    cap,
    step,
    owners,
    table,
    count,
    groups,
    lengths,
    cache,
    slot_len,
    listed,
    prefix_held,
    places,
    ahead,
    group_fill,
    found,
    sems,
):
    device = lax.axis_index("pool")
    home_count = owners
    row_count = groups.shape[0] // home_count
    group_id = device // DGRP
    prefill_id = device // PGRP
    blocks_here = listed.shape[0]
    most_blocks = table.shape[1]
    chunk = min(cap, step)

    def one_home(s, filled):
        here = jnp.int32(0)
        for i in range(row_count):
            row = s * row_count + i
            found[here] = lengths[row]
            here = here + (groups[row] == group_id).astype(jnp.int32)
        for c in range(cap):
            slot_len[s * cap + c] = jnp.where(c < here, found[c], 0)
        for b in range(cap // chunk):
            listed[1 + jnp.minimum(filled, blocks_here - 2)] = s * (cap // chunk) + b
            filled = filled + (here > b * chunk).astype(jnp.int32)
        return filled

    live = lax.fori_loop(0, home_count, one_home, jnp.int32(0))
    listed[0] = live
    for i in range(ahead.shape[0] // chunk):
        pl.when(i < live)(fetch_block(cache, listed, i, chunk, ahead, i, sems.at[i]).start)

    for a in range(owners // DGRP):
        group_fill[a] = 0
    for i in range(row_count):
        a = groups[device * row_count + i]
        c = group_fill[a]
        places[2 * i] = a
        places[2 * i + 1] = c
        group_fill[a] = c + 1

    def one_owner(o, carry):
        prefix_held[o] = 0
        return carry

    lax.fori_loop(0, owners, one_owner, 0, unroll=8)
    pool_blocks = prefix_held.shape[0] // owners

    def one_entry(j, carry):
        o = lax.div(table[prefill_id, j], pool_blocks)
        prefix_held[o] = prefix_held[o] + 1
        return carry

    lax.fori_loop(0, jnp.minimum(count[prefill_id], most_blocks), one_entry, 0)
    for i in range(ahead.shape[0] // chunk):
        pl.when(i < live)(fetch_block(cache, listed, i, chunk, ahead, i, sems.at[i]).wait)


def decode_kernel(
    cap, head_rows, chunk, width, listed, slot_len, recv, ahead, cache, out, held, sems
):
    pair_count, positions = cache.shape[1], cache.shape[2]
    per_home = cap // chunk
    key_count = pair_count * positions
    query_heads = head_rows // pair_count
    live = listed[0]
    scale = LANES ** (-0.5) * LOG2E
    rows = chunk * head_rows
    slots = width * chunk
    pair = 2 if chunk % 2 == 0 else 1

    def fetch(i):
        return fetch_block(cache, listed, i, chunk, held, i - width, sems.at[i - width])

    def begin(i, carry):
        fetch(i).start()
        return carry

    lax.fori_loop(width, live, begin, 0)
    row_pair = lax.broadcasted_iota(jnp.int32, (head_rows, key_count), 0) // query_heads
    key_axis = lax.broadcasted_iota(jnp.int32, (head_rows, key_count), 1)
    pos = jnp.where(key_axis // positions == row_pair, key_axis % positions, positions)
    half = head_rows // 2
    lane = lax.broadcasted_iota(jnp.int32, (half, LANES), 1)
    part, stat_slot = lane % (LANES // 2) % 3, lane % (LANES // 2) // 3

    def several(t, kv):
        ids = [jnp.minimum(t * width + w, live - 1) for w in range(width)]
        blocks = [listed[1 + i] for i in ids]
        homes = [b // per_home for b in blocks]
        firsts = [(b % per_home) * chunk for b in blocks]
        places = [pl.multiple_of(f * head_rows, 16) for f in firsts]
        q = jnp.concatenate(
            [recv[h, pl.ds(p, rows), :] for h, p in zip(homes, places)], axis=0
        )
        keys = kv[..., :LANES].reshape(slots, key_count, LANES)
        values = kv[..., LANES:].reshape(slots, key_count, LANES)
        scores = jnp.einsum(
            "jqd,jkd->jqk",
            q.reshape(slots // pair, pair * head_rows, LANES),
            keys.reshape(slots // pair, pair * key_count, LANES),
            preferred_element_type=jnp.float32,
        )
        if pair == 2:
            scores = jnp.stack(
                [scores[:, :head_rows, :key_count], scores[:, head_rows:, key_count:]], axis=1
            ).reshape(slots, head_rows, key_count)
        kept = jnp.stack(
            [pos < slot_len[blocks[w] * chunk + j] for w in range(width) for j in range(chunk)]
        )
        scores = jnp.where(kept, scores, MASKED)
        top = jnp.max(scores, axis=2, keepdims=True)
        weights = jnp.exp2((scores - top) * scale)
        total = jnp.sum(weights, axis=2, keepdims=True)
        weights = weights.astype(jnp.bfloat16)
        if pair == 2:
            weights = weights.reshape(slots // 2, 2, head_rows, key_count)
            nothing = jnp.zeros((slots // 2, head_rows, key_count), jnp.bfloat16)
            upper = jnp.concatenate([weights[:, 0], nothing], axis=2)
            lower = jnp.concatenate([nothing, weights[:, 1]], axis=2)
            weights = jnp.concatenate([upper, lower], axis=1)
        mixed = jnp.einsum(
            "jqk,jkd->jqd",
            weights,
            values.reshape(slots // pair, pair * key_count, LANES),
            preferred_element_type=jnp.float32,
        )
        mixed = mixed.reshape(slots, head_rows, LANES) / total
        mass = top * scale + jnp.log(total) * LOG2E
        high = mass.astype(jnp.bfloat16).astype(jnp.float32)
        middle = (mass - high).astype(jnp.bfloat16).astype(jnp.float32)
        low = mass - high - middle
        mixed = mixed.reshape(width, rows, LANES)
        for w in reversed(range(width)):
            out[homes[w], pl.ds(places[w], rows), :] = mixed[w].astype(out.dtype)
            masses = out[homes[w], cap * head_rows :, :].astype(jnp.float32)
            for j in range(chunk):
                at = w * chunk + j
                split = [
                    jnp.where(lane < LANES // 2, piece[at, :half], piece[at, half:])
                    for piece in (high, middle, low)
                ]
                split = jnp.where(part == 0, split[0], jnp.where(part == 1, split[1], split[2]))
                masses = jnp.where(stat_slot == firsts[w] + j, split, masses)
            out[homes[w], cap * head_rows :, :] = masses.astype(out.dtype)

    several(0, ahead[...])

    def later(t, carry):
        for w in range(width):
            pl.when(t * width + w < live)(fetch(t * width + w).wait)
        several(t, held[pl.ds((t - 1) * slots, slots)])
        return carry

    lax.fori_loop(1, (live + width - 1) // width, later, 0)


def prefill_kernel(planes, tile, prefix_held, *rest):
    sources = rest[:planes]
    q, new_kv, out, keys, values = rest[planes:]
    blk = sources[0].shape[2]
    prefix = planes * PLANE * PCAP * blk
    token_count = new_kv.shape[0]
    scale = LANES ** (-0.5) * LOG2E
    device = lax.axis_index("pool")

    @pl.when(pl.program_id(0) == 0)
    def _():
        first = jnp.broadcast_to(new_kv[0:1, :LANES], (blk, LANES))
        ones = jnp.ones((blk, LANES), values.dtype)
        for step in range(planes):
            sender = device // PLANE
            sender = sender ^ step if planes & (planes - 1) == 0 else (sender + planes - step) % planes
            for t in range(PLANE):
                owner = sender * PLANE + ((device % PLANE) ^ t)
                for k in range(PCAP):
                    ordinal = (step * PLANE + t) * PCAP + k
                    block = sources[step][t, k]
                    at = slice(ordinal * blk, (ordinal + 1) * blk)
                    here = prefix_held[owner] > k
                    keys[at, :] = jnp.where(here, block[:, :LANES], first)
                    values[at, :LANES] = jnp.where(here, block[:, LANES:], jnp.zeros_like(ones))
                    values[at, LANES:] = jnp.where(here, ones, jnp.zeros_like(ones))
        keys[prefix:, :] = new_kv[:, :LANES]
        values[prefix:, :LANES] = new_kv[:, LANES:]
        values[prefix:, LANES:] = jnp.ones((token_count, LANES), values.dtype)

    for t in range(token_count // tile):
        width = prefix + (t + 1) * tile
        block = q[t * tile : (t + 1) * tile, :]
        scores = lax.dot_general(
            block, keys[:width, :], (((1,), (1,)), ((), ())), preferred_element_type=jnp.float32
        )
        causal = lax.broadcasted_iota(jnp.int32, (tile, tile), 0) >= lax.broadcasted_iota(
            jnp.int32, (tile, tile), 1
        )
        scores = jnp.concatenate(
            [scores[:, : width - tile], jnp.where(causal, scores[:, width - tile :], MASKED)], axis=1
        )
        top = jnp.max(scores, axis=1, keepdims=True)
        weights = jnp.exp2((scores - top) * scale)
        mixed = jnp.dot(
            weights.astype(jnp.bfloat16), values[:width, :], preferred_element_type=jnp.float32
        )
        out[t * tile : (t + 1) * tile, :] = (mixed[:, :LANES] / mixed[:, LANES:]).astype(out.dtype)


def own_kernel(q, kv, score, value, key):
    row_count = q.shape[0]
    head_total = q.shape[1] // LANES
    per_pair = head_total // (kv.shape[1] // (2 * LANES))
    for h in range(head_total):
        at = pl.ds(h, row_count, stride=head_total)
        lane = h // per_pair * 2 * LANES
        score[at, :] = q[:, h * LANES : (h + 1) * LANES].astype(jnp.float32)
        key[at, :] = kv[:, lane : lane + LANES].astype(jnp.float32)
        value[at, :] = kv[:, lane + LANES : lane + 2 * LANES].astype(jnp.float32)
    for i in range(row_count):
        at = slice(i * head_total, (i + 1) * head_total)
        product = jnp.sum(score[at, :] * key[at, :], axis=1, keepdims=True)
        score[at, :] = jnp.broadcast_to(product * (LANES ** (-0.5) * LOG2E), (head_total, LANES))


def unpack_kernel(cap, head_rows, places, back, score, value, out, rows_scr):
    row_count = out.shape[0]
    head_total = out.shape[1] // LANES
    lane = lax.broadcasted_iota(jnp.int32, (head_rows // 2, LANES), 1)
    stat_slot = lane % (LANES // 2) // 3
    for i in range(row_count):
        a, c = places[2 * i], places[2 * i + 1]
        for m in range(DGRP):
            at = slice(i * head_total + m * head_rows, i * head_total + (m + 1) * head_rows)
            cached = back[
                a * DGRP + m, pl.ds(pl.multiple_of(c * head_rows, 16), head_rows), :
            ].astype(jnp.float32)
            masses = back[a * DGRP + m, cap * head_rows :, :].astype(jnp.float32)
            masses = jnp.where(stat_slot == c, masses, 0.0)
            mass = jnp.concatenate(
                [
                    jnp.sum(jnp.where(lane < LANES // 2, masses, 0.0), axis=1, keepdims=True),
                    jnp.sum(jnp.where(lane < LANES // 2, 0.0, masses), axis=1, keepdims=True),
                ],
                axis=0,
            )
            share = 1.0 / (1.0 + jnp.exp2(mass - score[at, :]))
            rows_scr[at, :] = cached + share * (value[at, :] - cached)
    for h in range(head_total):
        out[:, h * LANES : (h + 1) * LANES] = rows_scr[
            pl.ds(h, row_count, stride=head_total), :
        ].astype(out.dtype)


def shards(
    pool_kv,
    prefix_table,
    prefix_count,
    prefill_q,
    prefill_new_kv,
    decode_q,
    decode_new,
    decode_cache,
    decode_group,
    cached_len,
):
    devices = lax.axis_size("pool")
    blk = pool_kv.shape[2]
    row_count, q_width = decode_q.shape
    cap = decode_cache.shape[1] // devices
    decode_groups = devices // DGRP
    pair_count = decode_cache.shape[2]
    head_rows = q_width // LANES // DGRP
    message_rows = cap * head_rows
    groups = decode_group.reshape(-1)
    prefill_groups = prefix_table.shape[0]
    small = pltpu.CompilerParams(vmem_limit_bytes=8 * 2**20)

    share = jax.ShapeDtypeStruct(
        (PGRP // PLANE, prefill_groups, PCAP, blk, 2 * LANES), jnp.bfloat16
    )
    sending, *shares = pl.pallas_call(
        functools.partial(pack_kernel, head_rows),
        out_shape=(
            jax.ShapeDtypeStruct((decode_groups, DGRP, message_rows, LANES), jnp.bfloat16),
        )
        + (share,) * PLANE,
        in_specs=[smem_spec()] * 3 + [vmem_spec(), any_spec()],
        out_specs=(any_spec(),) * (1 + PLANE),
        scratch_shapes=[
            pltpu.VMEM((row_count * q_width // LANES, LANES), jnp.float32),
            pltpu.VMEM((DGRP, decode_groups, message_rows, LANES), jnp.bfloat16),
            pltpu.SMEM((decode_groups,), jnp.int32),
            pltpu.SemaphoreType.DMA((DGRP,)),
            pltpu.SemaphoreType.DMA((2 * PLANE * PCAP,)),
        ],
        compiler_params=small,
        name="pack",
    )(
        in_hbm(groups),
        in_hbm(prefix_table),
        in_hbm(prefix_count),
        in_hbm(decode_q),
        in_hbm(pool_kv.reshape((-1, PGRP // PLANE, PLANE) + pool_kv.shape[2:])),
    )
    sending = sending.reshape(devices, message_rows, LANES)

    received = lax.all_to_all(sending, "pool", split_axis=0, concat_axis=0, tiled=True)

    shares = [shares[0]] + [
        lax.ppermute(shares[t], "pool", [(i, i ^ t) for i in range(devices)])
        for t in range(1, PLANE)
    ]
    chunk = min(cap, 4)
    width = 8
    block_count = devices * cap // chunk
    slot_len, listed, prefix_held, places, ahead = pl.pallas_call(
        functools.partial(plan_kernel, cap, chunk, devices),
        out_shape=(
            jax.ShapeDtypeStruct((devices * cap,), jnp.int32),
            jax.ShapeDtypeStruct((block_count + 2,), jnp.int32),
            jax.ShapeDtypeStruct((devices * pool_kv.shape[0],), jnp.int32),
            jax.ShapeDtypeStruct((2 * row_count,), jnp.int32),
            jax.ShapeDtypeStruct((width * chunk,) + decode_cache.shape[2:], jnp.bfloat16),
        ),
        in_specs=[smem_spec()] * 4 + [any_spec()],
        out_specs=(smem_spec(),) * 4 + (vmem_spec(),),
        scratch_shapes=[
            pltpu.SMEM((decode_groups,), jnp.int32),
            pltpu.SMEM((cap + 1,), jnp.int32),
            pltpu.SemaphoreType.DMA((width,)),
        ],
        compiler_params=small,
        cost_estimate=pl.CostEstimate(flops=1000000, bytes_accessed=4000000, transcendentals=0),
        name="plan",
    )(in_hbm(prefix_table), in_hbm(prefix_count), in_hbm(groups), in_hbm(cached_len), in_hbm(decode_cache[0]))

    *shares, slot_len, listed = lax.optimization_barrier((*shares, slot_len, listed))
    planes = devices // PLANE
    bundle = jax.ShapeDtypeStruct((PLANE, PCAP, blk, 2 * LANES), jnp.bfloat16)
    bundles = pl.pallas_call(
        functools.partial(regroup_kernel, planes),
        out_shape=(bundle,) * planes,
        in_specs=[any_spec()] * PLANE,
        out_specs=(any_spec(),) * planes,
        scratch_shapes=[pltpu.SemaphoreType.DMA((planes * PLANE,))],
        compiler_params=small,
        cost_estimate=pl.CostEstimate(flops=100000, bytes_accessed=1000000, transcendentals=0),
        name="regroup",
    )(*shares)

    def along_line(step):
        pairs = [
            (i, partner(i // PLANE, step, planes) * PLANE + i % PLANE) for i in range(devices)
        ]
        return lax.ppermute(bundles[step], "pool", pairs)


    far_first = {step: along_line(step) for step in reversed(range(1, planes))}
    lines = [bundles[0]] + [far_first[step] for step in range(1, planes)]

    answers = pl.pallas_call(
        functools.partial(decode_kernel, cap, head_rows, chunk, width),
        out_shape=jax.ShapeDtypeStruct(
            (devices, cap * head_rows + head_rows // 2, LANES), jnp.bfloat16
        ),
        in_specs=[smem_spec(), smem_spec(), vmem_spec(), vmem_spec(), any_spec()],
        out_specs=vmem_spec(),
        scratch_shapes=[
            pltpu.VMEM(((block_count - width) * chunk,) + decode_cache.shape[2:], jnp.bfloat16),
            pltpu.SemaphoreType.DMA((block_count - width,)),
        ],
        compiler_params=pltpu.CompilerParams(vmem_limit_bytes=20 * 2**20),
        cost_estimate=pl.CostEstimate(
            flops=500000000, bytes_accessed=8000000, transcendentals=1000000
        ),
        name="decode",
    )(listed, slot_len, received, ahead, in_hbm(decode_cache[0]))

    back = lax.all_to_all(answers, "pool", split_axis=0, concat_axis=0, tiled=True)

    token_count, fill_width = prefill_q.shape[1:]
    prefix = devices * PCAP * blk
    head_count = fill_width // LANES
    prefix_held, decode_q, decode_new, _ = lax.optimization_barrier(
        (prefix_held, decode_q, decode_new, answers)
    )
    expanded = jax.ShapeDtypeStruct((row_count * q_width // LANES, LANES), jnp.float32)
    own_score, own_value = pl.pallas_call(
        own_kernel,
        out_shape=(expanded, expanded),
        in_specs=[vmem_spec(), vmem_spec()],
        out_specs=(vmem_spec(), vmem_spec()),
        scratch_shapes=[pltpu.VMEM(expanded.shape, jnp.float32)],
        compiler_params=small,
        cost_estimate=pl.CostEstimate(flops=1000000, bytes_accessed=2000000, transcendentals=0),
        name="own",
    )(in_hbm(decode_q), in_hbm(decode_new))
    prefill_out = pl.pallas_call(
        functools.partial(prefill_kernel, planes, min(256, token_count)),
        grid=(head_count,),
        out_shape=jax.ShapeDtypeStruct((token_count, fill_width), jnp.bfloat16),
        in_specs=[smem_spec()]
        + [pl.BlockSpec(bundle.shape, lambda u: (0, 0, 0, 0))] * planes
        + [
            pl.BlockSpec((token_count, LANES), lambda u: (0, u)),
            pl.BlockSpec(prefill_new_kv.shape[1:], lambda u: (0, 0)),
        ],
        out_specs=pl.BlockSpec((token_count, LANES), lambda u: (0, u)),
        scratch_shapes=[
            pltpu.VMEM((prefix + token_count, LANES), jnp.bfloat16),
            pltpu.VMEM((prefix + token_count, 2 * LANES), jnp.bfloat16),
        ],
        compiler_params=pltpu.CompilerParams(vmem_limit_bytes=16 * 2**20),
        cost_estimate=pl.CostEstimate(
            flops=32 * token_count * fill_width * (prefix + token_count),
            bytes_accessed=3000000,
            transcendentals=token_count * head_count * (prefix + token_count // 2),
        ),
        name="prefill",
    )(prefix_held, *lines, in_hbm(prefill_q[0]), in_hbm(prefill_new_kv[0]))

    decode_out = pl.pallas_call(
        functools.partial(unpack_kernel, cap, head_rows),
        out_shape=jax.ShapeDtypeStruct((row_count, q_width), jnp.bfloat16),
        in_specs=[smem_spec()] + [vmem_spec()] * 3,
        out_specs=vmem_spec(),
        scratch_shapes=[pltpu.VMEM(expanded.shape, jnp.float32)],
        compiler_params=small,
        name="unpack",
    )(places, back, own_score, own_value)
    return (prefill_out[None], decode_out)


def solution(mesh):
    in_specs = (
        P(("rep", "pool"), None, None, None),
        P("rep", None),
        P("rep"),
        P(("rep", "pool"), None, None),
        P(("rep", "pool"), None, None),
        P(("rep", "pool"), None),
        P(("rep", "pool"), None),
        P(("rep", "pool"), None, None, None, None),
        P("rep", None),
        P("rep"),
    )
    out_specs = (P(("rep", "pool"), None, None), P(("rep", "pool"), None))
    return jax.shard_map(shards, mesh=mesh, in_specs=in_specs, out_specs=out_specs, check_vma=False)
```

profile of v0, /device:TPU:0, one launch (start us, length us, event | category | flops | bytes accessed | tf_op | source)
XLA Modules:
  0.0 53.5 jit_solution(15319021576070540510)
XLA Ops:
  0.6 3.0 %pack.1 = (bf16[4,4,128,128]{3,2,1,0:T(8,128)(2,1)}, bf16[2,2,2,16,256]{4,3,2,1,0:T(8,128)(2,1)S(1)}, bf16[2,2,2,16,256]{4,3,2,1,0:T(8,128)(2,1)S(1)}, bf16[2,2,...) custom-call(s32[256]{0:T(256)} %bitcast.10, s32[2,32]{1,0:T(2,128)} %table.3, s32[2]{0:T(128)} %count.3, ...), custom_call_target="tpu_custom_call" | custom-call | tf_op jit(solution)/shard_map/pack/pallas_call | solution.py:426
  3.7 7.4 %all-to-all-start = ((bf16[16,128,128]{2,1,0:T(8,128)(2,1)}), bf16[16,128,128]{2,1,0:T(8,128)(2,1)S(1)}, u32[]{:S(2)}, u32[]{:S(2)}) async-start(bf16[16,128,128]{2,1,0:T(8,128)(2,1)} %bitcast.3), calls=%async_computation | async-start | bytes 1048576 | tf_op jit(solution)/shard_map/all_to_all | solution.py:452
  11.1 0.4 collective-permute-start
  11.5 1.7 %collective-permute-start.1 = (bf16[2,2,2,16,256]{4,3,2,1,0:T(8,128)(2,1)S(1)}, bf16[2,2,2,16,256]{4,3,2,1,0:T(8,128)(2,1)S(1)}, u32[]{:S(2)}, u32[]{:S(2)}) collective-permute-start(bf16[2,2,2,16,256]{4,3,2,1,0:T(8,128)(2,1)S(1)} %get-tuple-element.30), channel_id=1, source_target_pairs={{0,2},{1,3},{2,0},{3,1},{4,6},{5,7},{6,4},{7,5},{8,10},{9,11},{10,... | collective-permute-start | bytes 196616 | tf_op jit(solution)/shard_map/ppermute | solution.py:455
  13.2 0.0 collective-permute-start.2
  13.2 3.9 %plan.1 = (s32[128]{0:T(128)S(1)}, s32[34]{0:T(128)S(1)}, s32[64]{0:T(128)S(1)}, s32[32]{0:T(128)S(1)}, bf16[32,2,64,256]{3,2,1,0:T(8,128)(2,1)S(1)}) custom-call(s32[2,32]{1,0:T(2,128)} %table.3, s32[2]{0:T(128)} %count.3, s32[256]{0:T(256)} %bitcast.11, s32[256]{0:T(256)} %lengths.1, bf16[128,2,64,256]{3,2,1,0:T(8,128)(2,1)} %bitcast.7), custom_call_target="tpu_custom_call" | custom-call | flops 1000000 | bytes 4000000 | tf_op jit(solution)/shard_map/plan/pallas_call | solution.py:461
  17.1 0.0 collective-permute-done.rest_1_
  17.1 2.5 %collective-permute-done.1.rest_2_ = bf16[2,2,2,16,256]{4,3,2,1,0:T(8,128)(2,1)S(1)} collective-permute-done((bf16[2,2,2,16,256]{4,3,2,1,0:T(8,128)(2,1)S(1)}, bf16[2,2,2,16,256]{4,3,2,1,0:T(8,128)(2,1)S(1)}, u32[]{:S(2)}, u32[]{:S(2)}) %collective-permute-start.1) | collective-permute-done | bytes 65568 | tf_op jit(solution)/shard_map/ppermute | solution.py:455
  19.6 0.5 collective-permute-done.2.rest_3_
  20.0 0.5 regroup.1
  20.6 1.4 %collective-permute-start.3 = (bf16[4,2,16,256]{3,2,1,0:T(8,128)(2,1)S(1)}, bf16[4,2,16,256]{3,2,1,0:T(8,128)(2,1)S(1)}, u32[]{:S(2)}, u32[]{:S(2)}) collective-permute-start(bf16[4,2,16,256]{3,2,1,0:T(8,128)(2,1)S(1)} %get-tuple-element.44), channel_id=1, source_target_pairs={{0,4},{1,5},{2,6},{3,7},{4,0},{5,1},{6,2},{7,3},{8,12},{9,13},{10,... | collective-permute-start | bytes 196616 | tf_op jit(solution)/shard_map/ppermute | solution.py:500
  21.9 3.8 %collective-permute-start.4 = (bf16[4,2,16,256]{3,2,1,0:T(8,128)(2,1)S(1)}, bf16[4,2,16,256]{3,2,1,0:T(8,128)(2,1)S(1)}, u32[]{:S(2)}, u32[]{:S(2)}) collective-permute-start(bf16[4,2,16,256]{3,2,1,0:T(8,128)(2,1)S(1)} %get-tuple-element.45), channel_id=1, source_target_pairs={{0,8},{1,9},{2,10},{3,11},{4,12},{5,13},{6,14},{7,15},{8,0},{9,1},... | collective-permute-start | bytes 196616 | tf_op jit(solution)/shard_map/ppermute | solution.py:500
  25.7 0.0 collective-permute-start.5
  25.7 0.0 all-to-all-done.recv
  25.7 3.9 %decode.1 = bf16[16,136,128]{2,1,0:T(8,128)(2,1)} custom-call(s32[34]{0:T(128)S(1)} %get-tuple-element.34.listed, s32[128]{0:T(128)S(1)} %get-tuple-element.35.slot_len, bf16[16,128,128]{2,1,0:T(8,128)(2,1)S(1)} %all-to-all-done.recv, bf16[32,2,64,256]{3,2,1,0:T(8,128)(2,1)S(1)} %get-tuple-element.37.ahead, bf16[128,2,64,256]{3,2,1,0:T(8,128)(2,1)} %bitcast.8), custom_call_target="tpu_custom_call" | custom-call | flops 500000000 | bytes 8000000 | tf_op jit(solution)/shard_map/decode/pallas_call | solution.py:506
  29.6 6.9 %all-to-all-start.1 = ((bf16[16,136,128]{2,1,0:T(8,128)(2,1)}), bf16[16,136,128]{2,1,0:T(8,128)(2,1)S(1)}, u32[]{:S(2)}, u32[]{:S(2)}) async-start(bf16[16,136,128]{2,1,0:T(8,128)(2,1)} %decode.1), calls=%async_computation.1 | async-start | bytes 1114112 | tf_op jit(solution)/shard_map/all_to_all | solution.py:524
  36.5 2.2 %own.1 = (f32[1024,128]{1,0:T(8,128)S(1)}, f32[1024,128]{1,0:T(8,128)S(1)}) custom-call(bf16[16,8192]{1,0:T(8,128)(2,1)} %q.2, bf16[16,2048]{1,0:T(8,128)(2,1)} %kv), custom_call_target="tpu_custom_call" | custom-call | flops 1000000 | bytes 2000000 | tf_op jit(solution)/shard_map/own/pallas_call | solution.py:533
  38.6 0.0 collective-permute-done.3.rest_1_
  38.6 0.0 collective-permute-done.4.rest_2_
  38.7 0.0 collective-permute-done.5.rest_3_
  38.7 11.9 %prefill.1 = bf16[512,1024]{1,0:T(8,128)(2,1)} custom-call(s32[64]{0:T(128)S(1)} %get-tuple-element.38.prefix_held, bf16[4,2,16,256]{3,2,1,0:T(8,128)(2,1)S(1)} %get-tuple-element.43.rest_0_, bf16[4,2,16,256]{3,2,1,0:T(8,128)(2,1)S(1)} %collective-permute-done.3.rest_1_, bf16[4,2,16,256]{3,2,1,0:T(8,128)(2,1)S(1)} %collective-permute-done.4.rest_2_, ...), custom_call_target="tpu_custom_call" | custom-call | flops 17179869184 | bytes 3000000 | tf_op jit(solution)/shard_map/prefill/pallas_call | solution.py:543
  50.6 0.9 %all-to-all-done.1.back = bf16[16,136,128]{2,1,0:T(8,128)(2,1)S(1)} async-done(((bf16[16,136,128]{2,1,0:T(8,128)(2,1)}), bf16[16,136,128]{2,1,0:T(8,128)(2,1)S(1)}, u32[]{:S(2)}, u32[]{:S(2)}) %all-to-all-start.1) | async-done | bytes 557088 | tf_op jit(solution)/shard_map/all_to_all | solution.py:524
  51.5 2.0 %unpack.1 = bf16[16,8192]{1,0:T(8,128)(2,1)} custom-call(s32[32]{0:T(128)S(1)} %get-tuple-element.47.places, bf16[16,136,128]{2,1,0:T(8,128)(2,1)S(1)} %all-to-all-done.1.back, f32[1024,128]{1,0:T(8,128)S(1)} %get-tuple-element.50.score, f32[1024,128]{1,0:T(8,128)S(1)} %get-tuple-element.51.value), custom_call_target="tpu_custom_call" | custom-call | tf_op jit(solution)/shard_map/unpack/pallas_call | solution.py:567
Async XLA Ops:
  3.7 22.0 %all-to-all-start = ((bf16[16,128,128]{2,1,0:T(8,128)(2,1)}), bf16[16,128,128]{2,1,0:T(8,128)(2,1)S(1)}, u32[]{:S(2)}, u32[]{:S(2)}) async-start(bf16[16,128,128]{2,1,0:T(8,128)(2,1)} %bitcast.3), calls=%async_computation | async-start | bytes 1048576 | tf_op jit(solution)/shard_map/all_to_all | solution.py:452
  11.1 6.0 %collective-permute-start = (bf16[2,2,2,16,256]{4,3,2,1,0:T(8,128)(2,1)S(1)}, bf16[2,2,2,16,256]{4,3,2,1,0:T(8,128)(2,1)S(1)}, u32[]{:S(2)}, u32[]{:S(2)}) collective-permute-start(bf16[2,2,2,16,256]{4,3,2,1,0:T(8,128)(2,1)S(1)} %get-tuple-element.29), channel_id=1, source_target_pairs={{0,1},{1,0},{2,3},{3,2},{4,5},{5,4},{6,7},{7,6},{8,9},{9,8},{10,11... | collective-permute-start | bytes 196616 | tf_op jit(solution)/shard_map/ppermute | solution.py:455
  11.5 8.1 %collective-permute-start.1 = (bf16[2,2,2,16,256]{4,3,2,1,0:T(8,128)(2,1)S(1)}, bf16[2,2,2,16,256]{4,3,2,1,0:T(8,128)(2,1)S(1)}, u32[]{:S(2)}, u32[]{:S(2)}) collective-permute-start(bf16[2,2,2,16,256]{4,3,2,1,0:T(8,128)(2,1)S(1)} %get-tuple-element.30), channel_id=1, source_target_pairs={{0,2},{1,3},{2,0},{3,1},{4,6},{5,7},{6,4},{7,5},{8,10},{9,11},{10,... | collective-permute-start | bytes 196616 | tf_op jit(solution)/shard_map/ppermute | solution.py:455
  13.2 6.9 %collective-permute-start.2 = (bf16[2,2,2,16,256]{4,3,2,1,0:T(8,128)(2,1)S(1)}, bf16[2,2,2,16,256]{4,3,2,1,0:T(8,128)(2,1)S(1)}, u32[]{:S(2)}, u32[]{:S(2)}) collective-permute-start(bf16[2,2,2,16,256]{4,3,2,1,0:T(8,128)(2,1)S(1)} %get-tuple-element.31), channel_id=1, source_target_pairs={{0,3},{1,2},{2,1},{3,0},{4,7},{5,6},{6,5},{7,4},{8,11},{9,10},{10,... | collective-permute-start | bytes 196616 | tf_op jit(solution)/shard_map/ppermute | solution.py:455
  20.6 18.1 %collective-permute-start.3 = (bf16[4,2,16,256]{3,2,1,0:T(8,128)(2,1)S(1)}, bf16[4,2,16,256]{3,2,1,0:T(8,128)(2,1)S(1)}, u32[]{:S(2)}, u32[]{:S(2)}) collective-permute-start(bf16[4,2,16,256]{3,2,1,0:T(8,128)(2,1)S(1)} %get-tuple-element.44), channel_id=1, source_target_pairs={{0,4},{1,5},{2,6},{3,7},{4,0},{5,1},{6,2},{7,3},{8,12},{9,13},{10,... | collective-permute-start | bytes 196616 | tf_op jit(solution)/shard_map/ppermute | solution.py:500
  21.9 16.7 %collective-permute-start.4 = (bf16[4,2,16,256]{3,2,1,0:T(8,128)(2,1)S(1)}, bf16[4,2,16,256]{3,2,1,0:T(8,128)(2,1)S(1)}, u32[]{:S(2)}, u32[]{:S(2)}) collective-permute-start(bf16[4,2,16,256]{3,2,1,0:T(8,128)(2,1)S(1)} %get-tuple-element.45), channel_id=1, source_target_pairs={{0,8},{1,9},{2,10},{3,11},{4,12},{5,13},{6,14},{7,15},{8,0},{9,1},... | collective-permute-start | bytes 196616 | tf_op jit(solution)/shard_map/ppermute | solution.py:500
  25.7 13.0 %collective-permute-start.5 = (bf16[4,2,16,256]{3,2,1,0:T(8,128)(2,1)S(1)}, bf16[4,2,16,256]{3,2,1,0:T(8,128)(2,1)S(1)}, u32[]{:S(2)}, u32[]{:S(2)}) collective-permute-start(bf16[4,2,16,256]{3,2,1,0:T(8,128)(2,1)S(1)} %get-tuple-element.46), channel_id=1, source_target_pairs={{0,12},{1,13},{2,14},{3,15},{4,8},{5,9},{6,10},{7,11},{8,4},{9,5},... | collective-permute-start | bytes 196616 | tf_op jit(solution)/shard_map/ppermute | solution.py:500
  29.6 21.9 %all-to-all-start.1 = ((bf16[16,136,128]{2,1,0:T(8,128)(2,1)}), bf16[16,136,128]{2,1,0:T(8,128)(2,1)S(1)}, u32[]{:S(2)}, u32[]{:S(2)}) async-start(bf16[16,136,128]{2,1,0:T(8,128)(2,1)} %decode.1), calls=%async_computation.1 | async-start | bytes 1114112 | tf_op jit(solution)/shard_map/all_to_all | solution.py:524
where the time goes:
time: 53.9 us; the launch traced here: 53.5 us
  Pallas kernels  27.4 us (51%)
  starting transfers between devices  21.5 us (40%)
  waiting for transfers between devices  3.91 us (7%)
  between operations  0.72 us (1%)
    pallas_call x1, Pallas kernels, shards(): pl.pallas_call(functools.partial(prefill_kernel, planes, min(256, token_c...  11.9 us
    all_to_all x1, starting transfers between devices, shards(): lax.all_to_all(sending, 'pool', split_axis=0, concat_axis=0, tiled=True)  7.37 us
    all_to_all x1, starting transfers between devices, shards(): lax.all_to_all(answers, 'pool', split_axis=0, concat_axis=0, tiled=True)  6.87 us
    ppermute x3, starting transfers between devices, along_line(): return lax.ppermute(bundles[step], 'pool', pairs)  5.13 us
    pallas_call x1, Pallas kernels, shards(): pl.pallas_call(functools.partial(plan_kernel, cap, chunk, devices), out_s...  3.89 us
    pallas_call x1, Pallas kernels, shards(): pl.pallas_call(functools.partial(decode_kernel, cap, head_rows, chunk, wi...  3.88 us
    pallas_call x1, Pallas kernels, shards(): pl.pallas_call(functools.partial(pack_kernel, head_rows), out_shape=(jax....  3.05 us
    ppermute x3, waiting for transfers between devices, shards(): lax.ppermute(shares[t], 'pool', [(i, i ^ t) for i in range(devices)])  2.98 us
  transfers between devices with their start and end apart: 8, of which 3 were waited for; matrix products, arithmetic and copies ran while one was open for 0% of the time, Pallas kernels for 42%

commit v1 on v0

--- a/solution.py
+++ b/solution.py
@@ -32,9 +32,11 @@
     return pl.BlockSpec(memory_space=pltpu.VMEM)
 
 
-def pack_kernel(head_rows, groups, table, count, q, pool, out, *rest):
+def pack_kernel(head_rows, groups, table, count, q_far, pool, out, *rest):
     shares = rest[:PLANE]
-    rows_scr, stage, group_fill, sems, block_sems = rest[PLANE:]
+    q, rows_scr, stage, group_fill, sems, block_sems, q_sem = rest[PLANE:]
+    q_copy = pltpu.make_async_copy(q_far, q, q_sem)
+    q_copy.start()
     flying = send_blocks(table, count, pool, shares, block_sems)
     decode_groups = out.shape[0]
     row_count = q.shape[0]
@@ -42,16 +44,17 @@
     device = lax.axis_index("pool")
     for a in range(decode_groups):
         group_fill[a] = 0
-    for h in range(head_total):
-        rows_scr[pl.ds(h, row_count, stride=head_total), :] = q[
-            :, h * LANES : (h + 1) * LANES
-        ].astype(jnp.float32)
     homes = []
     for i in range(row_count):
         a = groups[device * row_count + i]
         c = group_fill[a]
         group_fill[a] = c + 1
         homes.append((a, c))
+    q_copy.wait()
+    for h in range(head_total):
+        rows_scr[pl.ds(h, row_count, stride=head_total), :] = q[
+            :, h * LANES : (h + 1) * LANES
+        ].astype(jnp.float32)
     copies = []
     for m in range(DGRP):
         for i, (a, c) in enumerate(homes):
@@ -303,7 +306,7 @@
 
 def prefill_kernel(planes, tile, prefix_held, *rest):
     sources = rest[:planes]
-    q, new_kv, out, keys, values = rest[planes:]
+    q, new_kv, out, keys, values, bias = rest[planes:]
     blk = sources[0].shape[2]
     prefix = planes * PLANE * PCAP * blk
     token_count = new_kv.shape[0]
@@ -312,8 +315,8 @@
 
     @pl.when(pl.program_id(0) == 0)
     def _():
-        first = jnp.broadcast_to(new_kv[0:1, :LANES], (blk, LANES))
-        ones = jnp.ones((blk, LANES), values.dtype)
+        lane_block = lax.broadcasted_iota(jnp.int32, (8, prefix), 1) // blk
+        hide = jnp.zeros((8, prefix), jnp.float32)
         for step in range(planes):
             sender = device // PLANE
             sender = sender ^ step if planes & (planes - 1) == 0 else (sender + planes - step) % planes
@@ -322,14 +325,13 @@
                 for k in range(PCAP):
                     ordinal = (step * PLANE + t) * PCAP + k
                     block = sources[step][t, k]
-                    at = slice(ordinal * blk, (ordinal + 1) * blk)
-                    here = prefix_held[owner] > k
-                    keys[at, :] = jnp.where(here, block[:, :LANES], first)
-                    values[at, :LANES] = jnp.where(here, block[:, LANES:], jnp.zeros_like(ones))
-                    values[at, LANES:] = jnp.where(here, ones, jnp.zeros_like(ones))
+                    keys[ordinal * blk : (ordinal + 1) * blk, :] = block[:, :LANES]
+                    values[ordinal * blk : (ordinal + 1) * blk, :] = block[:, LANES:]
+                    gone = jnp.where(prefix_held[owner] > k, 0.0, MASKED)
+                    hide = jnp.where(lane_block == ordinal, gone, hide)
+        bias[...] = hide
         keys[prefix:, :] = new_kv[:, :LANES]
-        values[prefix:, :LANES] = new_kv[:, LANES:]
-        values[prefix:, LANES:] = jnp.ones((token_count, LANES), values.dtype)
+        values[prefix:, :] = new_kv[:, LANES:]
 
     for t in range(token_count // tile):
         width = prefix + (t + 1) * tile
@@ -340,31 +342,35 @@
         causal = lax.broadcasted_iota(jnp.int32, (tile, tile), 0) >= lax.broadcasted_iota(
             jnp.int32, (tile, tile), 1
         )
-        scores = jnp.concatenate(
-            [scores[:, : width - tile], jnp.where(causal, scores[:, width - tile :], MASKED)], axis=1
-        )
+        pieces = [scores[:, :prefix] + bias[0:1, :]]
+        if t:
+            pieces.append(scores[:, prefix : width - tile])
+        pieces.append(jnp.where(causal, scores[:, width - tile :], MASKED))
+        scores = jnp.concatenate(pieces, axis=1)
         top = jnp.max(scores, axis=1, keepdims=True)
         weights = jnp.exp2((scores - top) * scale)
+        total = jnp.sum(weights, axis=1, keepdims=True)
         mixed = jnp.dot(
             weights.astype(jnp.bfloat16), values[:width, :], preferred_element_type=jnp.float32
         )
-        out[t * tile : (t + 1) * tile, :] = (mixed[:, :LANES] / mixed[:, LANES:]).astype(out.dtype)
-
-
-def own_kernel(q, kv, score, value, key):
+        out[t * tile : (t + 1) * tile, :] = (mixed / total).astype(out.dtype)
+
+
+def own_kernel(q, kv, score, value):
     row_count = q.shape[0]
     head_total = q.shape[1] // LANES
-    per_pair = head_total // (kv.shape[1] // (2 * LANES))
-    for h in range(head_total):
-        at = pl.ds(h, row_count, stride=head_total)
-        lane = h // per_pair * 2 * LANES
-        score[at, :] = q[:, h * LANES : (h + 1) * LANES].astype(jnp.float32)
-        key[at, :] = kv[:, lane : lane + LANES].astype(jnp.float32)
-        value[at, :] = kv[:, lane + LANES : lane + 2 * LANES].astype(jnp.float32)
-    for i in range(row_count):
-        at = slice(i * head_total, (i + 1) * head_total)
-        product = jnp.sum(score[at, :] * key[at, :], axis=1, keepdims=True)
-        score[at, :] = jnp.broadcast_to(product * (LANES ** (-0.5) * LOG2E), (head_total, LANES))
+    pair_count = kv.shape[1] // (2 * LANES)
+    per_pair = head_total // pair_count
+    for k in range(pair_count):
+        lane = k * 2 * LANES
+        key = kv[:, lane : lane + LANES].astype(jnp.float32) * (LANES ** (-0.5) * LOG2E)
+        held = kv[:, lane + LANES : lane + 2 * LANES].astype(jnp.float32)
+        for h in range(k * per_pair, (k + 1) * per_pair):
+            at = pl.ds(h, row_count, stride=head_total)
+            query = q[:, h * LANES : (h + 1) * LANES].astype(jnp.float32)
+            product = jnp.sum(query * key, axis=1, keepdims=True)
+            score[at, :] = jnp.broadcast_to(product, (row_count, LANES))
+            value[at, :] = held
 
 
 def unpack_kernel(cap, head_rows, places, back, score, value, out, rows_scr):
@@ -429,14 +435,16 @@
             jax.ShapeDtypeStruct((decode_groups, DGRP, message_rows, LANES), jnp.bfloat16),
         )
         + (share,) * PLANE,
-        in_specs=[smem_spec()] * 3 + [vmem_spec(), any_spec()],
+        in_specs=[smem_spec()] * 3 + [any_spec(), any_spec()],
         out_specs=(any_spec(),) * (1 + PLANE),
         scratch_shapes=[
+            pltpu.VMEM((row_count, q_width), jnp.bfloat16),
             pltpu.VMEM((row_count * q_width // LANES, LANES), jnp.float32),
             pltpu.VMEM((DGRP, decode_groups, message_rows, LANES), jnp.bfloat16),
             pltpu.SMEM((decode_groups,), jnp.int32),
             pltpu.SemaphoreType.DMA((DGRP,)),
             pltpu.SemaphoreType.DMA((2 * PLANE * PCAP,)),
+            pltpu.SemaphoreType.DMA,
         ],
         compiler_params=small,
         name="pack",
@@ -535,7 +543,6 @@
         out_shape=(expanded, expanded),
         in_specs=[vmem_spec(), vmem_spec()],
         out_specs=(vmem_spec(), vmem_spec()),
-        scratch_shapes=[pltpu.VMEM(expanded.shape, jnp.float32)],
         compiler_params=small,
         cost_estimate=pl.CostEstimate(flops=1000000, bytes_accessed=2000000, transcendentals=0),
         name="own",
@@ -553,7 +560,8 @@
         out_specs=pl.BlockSpec((token_count, LANES), lambda u: (0, u)),
         scratch_shapes=[
             pltpu.VMEM((prefix + token_count, LANES), jnp.bfloat16),
-            pltpu.VMEM((prefix + token_count, 2 * LANES), jnp.bfloat16),
+            pltpu.VMEM((prefix + token_count, LANES), jnp.bfloat16),
+            pltpu.VMEM((8, prefix), jnp.float32),
         ],
         compiler_params=pltpu.CompilerParams(vmem_limit_bytes=16 * 2**20),
         cost_estimate=pl.CostEstimate(

time: 53.9 us -> 53.4 us (level)
  waiting for transfers between devices: 3.91 us -> 5.02 us
  Pallas kernels: 27.4 us -> 26.4 us
    all_to_all x1, waiting for transfers between devices: 0.91 us -> 2.03 us  [shards(): lax.all_to_all(answers, 'pool', split_axis=0, concat_axis=0, tiled=True)]
    pallas_call x1, Pallas kernels: 11.9 us -> 11.1 us  [shards(): pl.pallas_call(functools.partial(prefill_kernel, planes, min(256, token_c...]
  transfers between devices with their start and end apart: 8 -> 8, of which waited for: 3 -> 3; matrix products, arithmetic and copies ran while one was open for 0% -> 0% of each run, Pallas kernels for 42% -> 40%
where the time goes in v1:
time: 53.4 us; the launch traced here: 53.2 us
  Pallas kernels  26.4 us (49%)
  starting transfers between devices  21.1 us (40%)
  waiting for transfers between devices  5.02 us (9%)
  between operations  0.72 us (1%)
    pallas_call x1, Pallas kernels, shards(): pl.pallas_call(functools.partial(prefill_kernel, planes, min(256, token_c...  11.1 us
    all_to_all x1, starting transfers between devices, shards(): lax.all_to_all(sending, 'pool', split_axis=0, concat_axis=0, tiled=True)  7.37 us
    all_to_all x1, starting transfers between devices, shards(): lax.all_to_all(answers, 'pool', split_axis=0, concat_axis=0, tiled=True)  6.48 us
    ppermute x3, starting transfers between devices, along_line(): return lax.ppermute(bundles[step], 'pool', pairs)  5.13 us
    pallas_call x1, Pallas kernels, shards(): pl.pallas_call(functools.partial(plan_kernel, cap, chunk, devices), out_s...  3.89 us
    pallas_call x1, Pallas kernels, shards(): pl.pallas_call(functools.partial(decode_kernel, cap, head_rows, chunk, wi...  3.88 us
    pallas_call x1, Pallas kernels, shards(): pl.pallas_call(functools.partial(pack_kernel, head_rows), out_shape=(jax....  3.11 us
    ppermute x3, waiting for transfers between devices, shards(): lax.ppermute(shares[t], 'pool', [(i, i ^ t) for i in range(devices)])  2.98 us
  transfers between devices with their start and end apart: 8, of which 3 were waited for; matrix products, arithmetic and copies ran while one was open for 0% of the time, Pallas kernels for 40%

profile of v1, /device:TPU:0, one launch (start us, length us, event | category | flops | bytes accessed | tf_op | source)
XLA Modules:
  0.0 53.2 jit_solution(18326972166952316752)
XLA Ops:
  0.6 3.1 %pack.1 = (bf16[4,4,128,128]{3,2,1,0:T(8,128)(2,1)}, bf16[2,2,2,16,256]{4,3,2,1,0:T(8,128)(2,1)S(1)}, bf16[2,2,2,16,256]{4,3,2,1,0:T(8,128)(2,1)S(1)}, bf16[2,2,...) custom-call(s32[256]{0:T(256)} %bitcast.10, s32[2,32]{1,0:T(2,128)} %table.3, s32[2]{0:T(128)} %count.3, ...), custom_call_target="tpu_custom_call" | custom-call | tf_op jit(solution)/shard_map/pack/pallas_call | solution.py:432
  3.7 7.4 %all-to-all-start = ((bf16[16,128,128]{2,1,0:T(8,128)(2,1)}), bf16[16,128,128]{2,1,0:T(8,128)(2,1)S(1)}, u32[]{:S(2)}, u32[]{:S(2)}) async-start(bf16[16,128,128]{2,1,0:T(8,128)(2,1)} %bitcast.3), calls=%async_computation | async-start | bytes 1048576 | tf_op jit(solution)/shard_map/all_to_all | solution.py:460
  11.1 0.4 collective-permute-start
  11.5 1.7 %collective-permute-start.1 = (bf16[2,2,2,16,256]{4,3,2,1,0:T(8,128)(2,1)S(1)}, bf16[2,2,2,16,256]{4,3,2,1,0:T(8,128)(2,1)S(1)}, u32[]{:S(2)}, u32[]{:S(2)}) collective-permute-start(bf16[2,2,2,16,256]{4,3,2,1,0:T(8,128)(2,1)S(1)} %get-tuple-element.30), channel_id=1, source_target_pairs={{0,2},{1,3},{2,0},{3,1},{4,6},{5,7},{6,4},{7,5},{8,10},{9,11},{10,... | collective-permute-start | bytes 196616 | tf_op jit(solution)/shard_map/ppermute | solution.py:463
  13.2 0.0 collective-permute-start.2
  13.2 3.9 %plan.1 = (s32[128]{0:T(128)S(1)}, s32[34]{0:T(128)S(1)}, s32[64]{0:T(128)S(1)}, s32[32]{0:T(128)S(1)}, bf16[32,2,64,256]{3,2,1,0:T(8,128)(2,1)S(1)}) custom-call(s32[2,32]{1,0:T(2,128)} %table.3, s32[2]{0:T(128)} %count.3, s32[256]{0:T(256)} %bitcast.11, s32[256]{0:T(256)} %lengths.1, bf16[128,2,64,256]{3,2,1,0:T(8,128)(2,1)} %bitcast.7), custom_call_target="tpu_custom_call" | custom-call | flops 1000000 | bytes 4000000 | tf_op jit(solution)/shard_map/plan/pallas_call | solution.py:469
  17.1 0.0 collective-permute-done.rest_1_
  17.1 2.5 %collective-permute-done.1.rest_2_ = bf16[2,2,2,16,256]{4,3,2,1,0:T(8,128)(2,1)S(1)} collective-permute-done((bf16[2,2,2,16,256]{4,3,2,1,0:T(8,128)(2,1)S(1)}, bf16[2,2,2,16,256]{4,3,2,1,0:T(8,128)(2,1)S(1)}, u32[]{:S(2)}, u32[]{:S(2)}) %collective-permute-start.1) | collective-permute-done | bytes 65568 | tf_op jit(solution)/shard_map/ppermute | solution.py:463
  19.6 0.5 collective-permute-done.2.rest_3_
  20.1 0.5 regroup.1
  20.6 1.4 %collective-permute-start.3 = (bf16[4,2,16,256]{3,2,1,0:T(8,128)(2,1)S(1)}, bf16[4,2,16,256]{3,2,1,0:T(8,128)(2,1)S(1)}, u32[]{:S(2)}, u32[]{:S(2)}) collective-permute-start(bf16[4,2,16,256]{3,2,1,0:T(8,128)(2,1)S(1)} %get-tuple-element.44), channel_id=1, source_target_pairs={{0,4},{1,5},{2,6},{3,7},{4,0},{5,1},{6,2},{7,3},{8,12},{9,13},{10,... | collective-permute-start | bytes 196616 | tf_op jit(solution)/shard_map/ppermute | solution.py:508
  22.0 3.8 %collective-permute-start.4 = (bf16[4,2,16,256]{3,2,1,0:T(8,128)(2,1)S(1)}, bf16[4,2,16,256]{3,2,1,0:T(8,128)(2,1)S(1)}, u32[]{:S(2)}, u32[]{:S(2)}) collective-permute-start(bf16[4,2,16,256]{3,2,1,0:T(8,128)(2,1)S(1)} %get-tuple-element.45), channel_id=1, source_target_pairs={{0,8},{1,9},{2,10},{3,11},{4,12},{5,13},{6,14},{7,15},{8,0},{9,1},... | collective-permute-start | bytes 196616 | tf_op jit(solution)/shard_map/ppermute | solution.py:508
  25.8 0.0 collective-permute-start.5
  25.8 0.0 all-to-all-done.recv
  25.8 3.9 %decode.1 = bf16[16,136,128]{2,1,0:T(8,128)(2,1)} custom-call(s32[34]{0:T(128)S(1)} %get-tuple-element.34.listed, s32[128]{0:T(128)S(1)} %get-tuple-element.35.slot_len, bf16[16,128,128]{2,1,0:T(8,128)(2,1)S(1)} %all-to-all-done.recv, bf16[32,2,64,256]{3,2,1,0:T(8,128)(2,1)S(1)} %get-tuple-element.37.ahead, bf16[128,2,64,256]{3,2,1,0:T(8,128)(2,1)} %bitcast.8), custom_call_target="tpu_custom_call" | custom-call | flops 500000000 | bytes 8000000 | tf_op jit(solution)/shard_map/decode/pallas_call | solution.py:514
  29.6 6.5 %all-to-all-start.1 = ((bf16[16,136,128]{2,1,0:T(8,128)(2,1)}), bf16[16,136,128]{2,1,0:T(8,128)(2,1)S(1)}, u32[]{:S(2)}, u32[]{:S(2)}) async-start(bf16[16,136,128]{2,1,0:T(8,128)(2,1)} %decode.1), calls=%async_computation.1 | async-start | bytes 1114112 | tf_op jit(solution)/shard_map/all_to_all | solution.py:532
  36.1 1.9 %own.1 = (f32[1024,128]{1,0:T(8,128)S(1)}, f32[1024,128]{1,0:T(8,128)S(1)}) custom-call(bf16[16,8192]{1,0:T(8,128)(2,1)} %q, bf16[16,2048]{1,0:T(8,128)(2,1)} %kv), custom_call_target="tpu_custom_call" | custom-call | flops 1000000 | bytes 2000000 | tf_op jit(solution)/shard_map/own/pallas_call | solution.py:541
  38.0 0.0 collective-permute-done.3.rest_1_
  38.0 0.0 collective-permute-done.4.rest_2_
  38.0 0.0 collective-permute-done.5.rest_3_
  38.0 11.1 %prefill.1 = bf16[512,1024]{1,0:T(8,128)(2,1)} custom-call(s32[64]{0:T(128)S(1)} %get-tuple-element.38.prefix_held, bf16[4,2,16,256]{3,2,1,0:T(8,128)(2,1)S(1)} %get-tuple-element.43.rest_0_, bf16[4,2,16,256]{3,2,1,0:T(8,128)(2,1)S(1)} %collective-permute-done.3.rest_1_, bf16[4,2,16,256]{3,2,1,0:T(8,128)(2,1)S(1)} %collective-permute-done.4.rest_2_, ...), custom_call_target="tpu_custom_call" | custom-call | flops 17179869184 | bytes 3000000 | tf_op jit(solution)/shard_map/prefill/pallas_call | solution.py:550
  49.1 2.0 %all-to-all-done.1.back = bf16[16,136,128]{2,1,0:T(8,128)(2,1)S(1)} async-done(((bf16[16,136,128]{2,1,0:T(8,128)(2,1)}), bf16[16,136,128]{2,1,0:T(8,128)(2,1)S(1)}, u32[]{:S(2)}, u32[]{:S(2)}) %all-to-all-start.1) | async-done | bytes 557088 | tf_op jit(solution)/shard_map/all_to_all | solution.py:532
  51.2 2.0 %unpack.1 = bf16[16,8192]{1,0:T(8,128)(2,1)} custom-call(s32[32]{0:T(128)S(1)} %get-tuple-element.47.places, bf16[16,136,128]{2,1,0:T(8,128)(2,1)S(1)} %all-to-all-done.1.back, f32[1024,128]{1,0:T(8,128)S(1)} %get-tuple-element.50.score, f32[1024,128]{1,0:T(8,128)S(1)} %get-tuple-element.51.value), custom_call_target="tpu_custom_call" | custom-call | tf_op jit(solution)/shard_map/unpack/pallas_call | solution.py:575
Async XLA Ops:
  3.7 22.0 %all-to-all-start = ((bf16[16,128,128]{2,1,0:T(8,128)(2,1)}), bf16[16,128,128]{2,1,0:T(8,128)(2,1)S(1)}, u32[]{:S(2)}, u32[]{:S(2)}) async-start(bf16[16,128,128]{2,1,0:T(8,128)(2,1)} %bitcast.3), calls=%async_computation | async-start | bytes 1048576 | tf_op jit(solution)/shard_map/all_to_all | solution.py:460
  11.1 6.0 %collective-permute-start = (bf16[2,2,2,16,256]{4,3,2,1,0:T(8,128)(2,1)S(1)}, bf16[2,2,2,16,256]{4,3,2,1,0:T(8,128)(2,1)S(1)}, u32[]{:S(2)}, u32[]{:S(2)}) collective-permute-start(bf16[2,2,2,16,256]{4,3,2,1,0:T(8,128)(2,1)S(1)} %get-tuple-element.29), channel_id=1, source_target_pairs={{0,1},{1,0},{2,3},{3,2},{4,5},{5,4},{6,7},{7,6},{8,9},{9,8},{10,11... | collective-permute-start | bytes 196616 | tf_op jit(solution)/shard_map/ppermute | solution.py:463
  11.5 8.1 %collective-permute-start.1 = (bf16[2,2,2,16,256]{4,3,2,1,0:T(8,128)(2,1)S(1)}, bf16[2,2,2,16,256]{4,3,2,1,0:T(8,128)(2,1)S(1)}, u32[]{:S(2)}, u32[]{:S(2)}) collective-permute-start(bf16[2,2,2,16,256]{4,3,2,1,0:T(8,128)(2,1)S(1)} %get-tuple-element.30), channel_id=1, source_target_pairs={{0,2},{1,3},{2,0},{3,1},{4,6},{5,7},{6,4},{7,5},{8,10},{9,11},{10,... | collective-permute-start | bytes 196616 | tf_op jit(solution)/shard_map/ppermute | solution.py:463
  13.2 6.9 %collective-permute-start.2 = (bf16[2,2,2,16,256]{4,3,2,1,0:T(8,128)(2,1)S(1)}, bf16[2,2,2,16,256]{4,3,2,1,0:T(8,128)(2,1)S(1)}, u32[]{:S(2)}, u32[]{:S(2)}) collective-permute-start(bf16[2,2,2,16,256]{4,3,2,1,0:T(8,128)(2,1)S(1)} %get-tuple-element.31), channel_id=1, source_target_pairs={{0,3},{1,2},{2,1},{3,0},{4,7},{5,6},{6,5},{7,4},{8,11},{9,10},{10,... | collective-permute-start | bytes 196616 | tf_op jit(solution)/shard_map/ppermute | solution.py:463
  20.6 17.4 %collective-permute-start.3 = (bf16[4,2,16,256]{3,2,1,0:T(8,128)(2,1)S(1)}, bf16[4,2,16,256]{3,2,1,0:T(8,128)(2,1)S(1)}, u32[]{:S(2)}, u32[]{:S(2)}) collective-permute-start(bf16[4,2,16,256]{3,2,1,0:T(8,128)(2,1)S(1)} %get-tuple-element.44), channel_id=1, source_target_pairs={{0,4},{1,5},{2,6},{3,7},{4,0},{5,1},{6,2},{7,3},{8,12},{9,13},{10,... | collective-permute-start | bytes 196616 | tf_op jit(solution)/shard_map/ppermute | solution.py:508
  22.0 16.0 %collective-permute-start.4 = (bf16[4,2,16,256]{3,2,1,0:T(8,128)(2,1)S(1)}, bf16[4,2,16,256]{3,2,1,0:T(8,128)(2,1)S(1)}, u32[]{:S(2)}, u32[]{:S(2)}) collective-permute-start(bf16[4,2,16,256]{3,2,1,0:T(8,128)(2,1)S(1)} %get-tuple-element.45), channel_id=1, source_target_pairs={{0,8},{1,9},{2,10},{3,11},{4,12},{5,13},{6,14},{7,15},{8,0},{9,1},... | collective-permute-start | bytes 196616 | tf_op jit(solution)/shard_map/ppermute | solution.py:508
  25.8 12.3 %collective-permute-start.5 = (bf16[4,2,16,256]{3,2,1,0:T(8,128)(2,1)S(1)}, bf16[4,2,16,256]{3,2,1,0:T(8,128)(2,1)S(1)}, u32[]{:S(2)}, u32[]{:S(2)}) collective-permute-start(bf16[4,2,16,256]{3,2,1,0:T(8,128)(2,1)S(1)} %get-tuple-element.46), channel_id=1, source_target_pairs={{0,12},{1,13},{2,14},{3,15},{4,8},{5,9},{6,10},{7,11},{8,4},{9,5},... | collective-permute-start | bytes 196616 | tf_op jit(solution)/shard_map/ppermute | solution.py:508
  29.6 21.5 %all-to-all-start.1 = ((bf16[16,136,128]{2,1,0:T(8,128)(2,1)}), bf16[16,136,128]{2,1,0:T(8,128)(2,1)S(1)}, u32[]{:S(2)}, u32[]{:S(2)}) async-start(bf16[16,136,128]{2,1,0:T(8,128)(2,1)} %decode.1), calls=%async_computation.1 | async-start | bytes 1114112 | tf_op jit(solution)/shard_map/all_to_all | solution.py:532

commit v2 on v1

--- a/solution.py
+++ b/solution.py
@@ -51,12 +51,12 @@
         group_fill[a] = c + 1
         homes.append((a, c))
     q_copy.wait()
-    for h in range(head_total):
-        rows_scr[pl.ds(h, row_count, stride=head_total), :] = q[
-            :, h * LANES : (h + 1) * LANES
-        ].astype(jnp.float32)
     copies = []
     for m in range(DGRP):
+        for h in range(m * head_rows, (m + 1) * head_rows):
+            rows_scr[pl.ds(h, row_count, stride=head_total), :] = q[
+                :, h * LANES : (h + 1) * LANES
+            ].astype(jnp.float32)
         for i, (a, c) in enumerate(homes):
             first = i * head_total + m * head_rows
             stage[m, a, pl.ds(pl.multiple_of(c * head_rows, 16), head_rows), :] = rows_scr[
@@ -373,14 +373,15 @@
             value[at, :] = held
 
 
-def unpack_kernel(cap, head_rows, places, back, score, value, out, rows_scr):
+def unpack_kernel(cap, head_rows, places, back, score, value, out, rows_scr, stage, sems):
     row_count = out.shape[0]
     head_total = out.shape[1] // LANES
     lane = lax.broadcasted_iota(jnp.int32, (head_rows // 2, LANES), 1)
     stat_slot = lane % (LANES // 2) // 3
-    for i in range(row_count):
-        a, c = places[2 * i], places[2 * i + 1]
-        for m in range(DGRP):
+    copies = []
+    for m in range(DGRP):
+        for i in range(row_count):
+            a, c = places[2 * i], places[2 * i + 1]
             at = slice(i * head_total + m * head_rows, i * head_total + (m + 1) * head_rows)
             cached = back[
                 a * DGRP + m, pl.ds(pl.multiple_of(c * head_rows, 16), head_rows), :
@@ -396,10 +397,16 @@
             )
             share = 1.0 / (1.0 + jnp.exp2(mass - score[at, :]))
             rows_scr[at, :] = cached + share * (value[at, :] - cached)
-    for h in range(head_total):
-        out[:, h * LANES : (h + 1) * LANES] = rows_scr[
-            pl.ds(h, row_count, stride=head_total), :
-        ].astype(out.dtype)
+        for h in range(m * head_rows, (m + 1) * head_rows):
+            stage[:, h * LANES : (h + 1) * LANES] = rows_scr[
+                pl.ds(h, row_count, stride=head_total), :
+            ].astype(out.dtype)
+        lanes = pl.ds(m * head_rows * LANES, head_rows * LANES)
+        copy = pltpu.make_async_copy(stage.at[:, lanes], out.at[:, lanes], sems.at[m])
+        copy.start()
+        copies.append(copy)
+    for copy in copies:
+        copy.wait()
 
 
 def shards(
@@ -576,8 +583,12 @@
         functools.partial(unpack_kernel, cap, head_rows),
         out_shape=jax.ShapeDtypeStruct((row_count, q_width), jnp.bfloat16),
         in_specs=[smem_spec()] + [vmem_spec()] * 3,
-        out_specs=vmem_spec(),
-        scratch_shapes=[pltpu.VMEM(expanded.shape, jnp.float32)],
+        out_specs=any_spec(),
+        scratch_shapes=[
+            pltpu.VMEM(expanded.shape, jnp.float32),
+            pltpu.VMEM((row_count, q_width), jnp.bfloat16),
+            pltpu.SemaphoreType.DMA((DGRP,)),
+        ],
         compiler_params=small,
         name="unpack",
     )(places, back, own_score, own_value)

time: 53.4 us -> 53.3 us (level)
  no operation moved by 1% of the time
where the time goes in v2:
time: 53.3 us; the launch traced here: 52.6 us
  Pallas kernels  26.2 us (49%)
  starting transfers between devices  20.6 us (39%)
  waiting for transfers between devices  5.02 us (9%)
  between operations  0.72 us (1%)
    pallas_call x1, Pallas kernels, shards(): pl.pallas_call(functools.partial(prefill_kernel, planes, min(256, token_c...  11.1 us
    all_to_all x1, starting transfers between devices, shards(): lax.all_to_all(sending, 'pool', split_axis=0, concat_axis=0, tiled=True)  7.37 us
    all_to_all x1, starting transfers between devices, shards(): lax.all_to_all(answers, 'pool', split_axis=0, concat_axis=0, tiled=True)  6.03 us
    ppermute x3, starting transfers between devices, along_line(): return lax.ppermute(bundles[step], 'pool', pairs)  5.13 us
    pallas_call x1, Pallas kernels, shards(): pl.pallas_call(functools.partial(plan_kernel, cap, chunk, devices), out_s...  3.89 us
    pallas_call x1, Pallas kernels, shards(): pl.pallas_call(functools.partial(decode_kernel, cap, head_rows, chunk, wi...  3.89 us
    pallas_call x1, Pallas kernels, shards(): pl.pallas_call(functools.partial(pack_kernel, head_rows), out_shape=(jax....  3.05 us
    ppermute x3, waiting for transfers between devices, shards(): lax.ppermute(shares[t], 'pool', [(i, i ^ t) for i in range(devices)])  2.98 us
  transfers between devices with their start and end apart: 8, of which 3 were waited for; matrix products, arithmetic and copies ran while one was open for 0% of the time, Pallas kernels for 40%

profile of v2, /device:TPU:0, one launch (start us, length us, event | category | flops | bytes accessed | tf_op | source)
XLA Modules:
  0.0 52.6 jit_solution(17969977477515409496)
XLA Ops:
  0.6 3.1 %pack.1 = (bf16[4,4,128,128]{3,2,1,0:T(8,128)(2,1)}, bf16[2,2,2,16,256]{4,3,2,1,0:T(8,128)(2,1)S(1)}, bf16[2,2,2,16,256]{4,3,2,1,0:T(8,128)(2,1)S(1)}, bf16[2,2,...) custom-call(s32[256]{0:T(256)} %bitcast.10, s32[2,32]{1,0:T(2,128)} %table.3, s32[2]{0:T(128)} %count.3, ...), custom_call_target="tpu_custom_call" | custom-call | tf_op jit(solution)/shard_map/pack/pallas_call | solution.py:439
  3.7 7.4 %all-to-all-start = ((bf16[16,128,128]{2,1,0:T(8,128)(2,1)}), bf16[16,128,128]{2,1,0:T(8,128)(2,1)S(1)}, u32[]{:S(2)}, u32[]{:S(2)}) async-start(bf16[16,128,128]{2,1,0:T(8,128)(2,1)} %bitcast.3), calls=%async_computation | async-start | bytes 1048576 | tf_op jit(solution)/shard_map/all_to_all | solution.py:467
  11.1 0.4 collective-permute-start
  11.5 1.7 %collective-permute-start.1 = (bf16[2,2,2,16,256]{4,3,2,1,0:T(8,128)(2,1)S(1)}, bf16[2,2,2,16,256]{4,3,2,1,0:T(8,128)(2,1)S(1)}, u32[]{:S(2)}, u32[]{:S(2)}) collective-permute-start(bf16[2,2,2,16,256]{4,3,2,1,0:T(8,128)(2,1)S(1)} %get-tuple-element.30), channel_id=1, source_target_pairs={{0,2},{1,3},{2,0},{3,1},{4,6},{5,7},{6,4},{7,5},{8,10},{9,11},{10,... | collective-permute-start | bytes 196616 | tf_op jit(solution)/shard_map/ppermute | solution.py:470
  13.2 0.0 collective-permute-start.2
  13.2 3.9 %plan.1 = (s32[128]{0:T(128)S(1)}, s32[34]{0:T(128)S(1)}, s32[64]{0:T(128)S(1)}, s32[32]{0:T(128)S(1)}, bf16[32,2,64,256]{3,2,1,0:T(8,128)(2,1)S(1)}) custom-call(s32[2,32]{1,0:T(2,128)} %table.3, s32[2]{0:T(128)} %count.3, s32[256]{0:T(256)} %bitcast.11, s32[256]{0:T(256)} %lengths.1, bf16[128,2,64,256]{3,2,1,0:T(8,128)(2,1)} %bitcast.7), custom_call_target="tpu_custom_call" | custom-call | flops 1000000 | bytes 4000000 | tf_op jit(solution)/shard_map/plan/pallas_call | solution.py:476
  17.1 0.0 collective-permute-done.rest_1_
  17.1 2.5 %collective-permute-done.1.rest_2_ = bf16[2,2,2,16,256]{4,3,2,1,0:T(8,128)(2,1)S(1)} collective-permute-done((bf16[2,2,2,16,256]{4,3,2,1,0:T(8,128)(2,1)S(1)}, bf16[2,2,2,16,256]{4,3,2,1,0:T(8,128)(2,1)S(1)}, u32[]{:S(2)}, u32[]{:S(2)}) %collective-permute-start.1) | collective-permute-done | bytes 65568 | tf_op jit(solution)/shard_map/ppermute | solution.py:470
  19.6 0.5 collective-permute-done.2.rest_3_
  20.1 0.5 regroup.1
  20.6 1.4 %collective-permute-start.3 = (bf16[4,2,16,256]{3,2,1,0:T(8,128)(2,1)S(1)}, bf16[4,2,16,256]{3,2,1,0:T(8,128)(2,1)S(1)}, u32[]{:S(2)}, u32[]{:S(2)}) collective-permute-start(bf16[4,2,16,256]{3,2,1,0:T(8,128)(2,1)S(1)} %get-tuple-element.44), channel_id=1, source_target_pairs={{0,4},{1,5},{2,6},{3,7},{4,0},{5,1},{6,2},{7,3},{8,12},{9,13},{10,... | collective-permute-start | bytes 196616 | tf_op jit(solution)/shard_map/ppermute | solution.py:515
  21.9 3.8 %collective-permute-start.4 = (bf16[4,2,16,256]{3,2,1,0:T(8,128)(2,1)S(1)}, bf16[4,2,16,256]{3,2,1,0:T(8,128)(2,1)S(1)}, u32[]{:S(2)}, u32[]{:S(2)}) collective-permute-start(bf16[4,2,16,256]{3,2,1,0:T(8,128)(2,1)S(1)} %get-tuple-element.45), channel_id=1, source_target_pairs={{0,8},{1,9},{2,10},{3,11},{4,12},{5,13},{6,14},{7,15},{8,0},{9,1},... | collective-permute-start | bytes 196616 | tf_op jit(solution)/shard_map/ppermute | solution.py:515
  25.7 0.0 collective-permute-start.5
  25.7 0.0 all-to-all-done.recv
  25.7 3.9 %decode.1 = bf16[16,136,128]{2,1,0:T(8,128)(2,1)} custom-call(s32[34]{0:T(128)S(1)} %get-tuple-element.34.listed, s32[128]{0:T(128)S(1)} %get-tuple-element.35.slot_len, bf16[16,128,128]{2,1,0:T(8,128)(2,1)S(1)} %all-to-all-done.recv, bf16[32,2,64,256]{3,2,1,0:T(8,128)(2,1)S(1)} %get-tuple-element.37.ahead, bf16[128,2,64,256]{3,2,1,0:T(8,128)(2,1)} %bitcast.8), custom_call_target="tpu_custom_call" | custom-call | flops 500000000 | bytes 8000000 | tf_op jit(solution)/shard_map/decode/pallas_call | solution.py:521
  29.6 6.0 %all-to-all-start.1 = ((bf16[16,136,128]{2,1,0:T(8,128)(2,1)}), bf16[16,136,128]{2,1,0:T(8,128)(2,1)S(1)}, u32[]{:S(2)}, u32[]{:S(2)}) async-start(bf16[16,136,128]{2,1,0:T(8,128)(2,1)} %decode.1), calls=%async_computation.1 | async-start | bytes 1114112 | tf_op jit(solution)/shard_map/all_to_all | solution.py:539
  35.6 1.9 %own.1 = (f32[1024,128]{1,0:T(8,128)S(1)}, f32[1024,128]{1,0:T(8,128)S(1)}) custom-call(bf16[16,8192]{1,0:T(8,128)(2,1)} %q, bf16[16,2048]{1,0:T(8,128)(2,1)} %kv), custom_call_target="tpu_custom_call" | custom-call | flops 1000000 | bytes 2000000 | tf_op jit(solution)/shard_map/own/pallas_call | solution.py:548
  37.5 0.0 collective-permute-done.3.rest_1_
  37.5 0.0 collective-permute-done.4.rest_2_
  37.5 0.0 collective-permute-done.5.rest_3_
  37.5 11.1 %prefill.1 = bf16[512,1024]{1,0:T(8,128)(2,1)} custom-call(s32[64]{0:T(128)S(1)} %get-tuple-element.38.prefix_held, bf16[4,2,16,256]{3,2,1,0:T(8,128)(2,1)S(1)} %get-tuple-element.43.rest_0_, bf16[4,2,16,256]{3,2,1,0:T(8,128)(2,1)S(1)} %collective-permute-done.3.rest_1_, bf16[4,2,16,256]{3,2,1,0:T(8,128)(2,1)S(1)} %collective-permute-done.4.rest_2_, ...), custom_call_target="tpu_custom_call" | custom-call | flops 17179869184 | bytes 3000000 | tf_op jit(solution)/shard_map/prefill/pallas_call | solution.py:557
  48.6 2.0 %all-to-all-done.1.back = bf16[16,136,128]{2,1,0:T(8,128)(2,1)S(1)} async-done(((bf16[16,136,128]{2,1,0:T(8,128)(2,1)}), bf16[16,136,128]{2,1,0:T(8,128)(2,1)S(1)}, u32[]{:S(2)}, u32[]{:S(2)}) %all-to-all-start.1) | async-done | bytes 557088 | tf_op jit(solution)/shard_map/all_to_all | solution.py:539
  50.7 1.9 %unpack.1 = bf16[16,8192]{1,0:T(8,128)(2,1)} custom-call(s32[32]{0:T(128)S(1)} %get-tuple-element.47.places, bf16[16,136,128]{2,1,0:T(8,128)(2,1)S(1)} %all-to-all-done.1.back, f32[1024,128]{1,0:T(8,128)S(1)} %get-tuple-element.50.score, f32[1024,128]{1,0:T(8,128)S(1)} %get-tuple-element.51.value), custom_call_target="tpu_custom_call" | custom-call | tf_op jit(solution)/shard_map/unpack/pallas_call | solution.py:582
Async XLA Ops:
  3.7 22.0 %all-to-all-start = ((bf16[16,128,128]{2,1,0:T(8,128)(2,1)}), bf16[16,128,128]{2,1,0:T(8,128)(2,1)S(1)}, u32[]{:S(2)}, u32[]{:S(2)}) async-start(bf16[16,128,128]{2,1,0:T(8,128)(2,1)} %bitcast.3), calls=%async_computation | async-start | bytes 1048576 | tf_op jit(solution)/shard_map/all_to_all | solution.py:467
  11.1 6.0 %collective-permute-start = (bf16[2,2,2,16,256]{4,3,2,1,0:T(8,128)(2,1)S(1)}, bf16[2,2,2,16,256]{4,3,2,1,0:T(8,128)(2,1)S(1)}, u32[]{:S(2)}, u32[]{:S(2)}) collective-permute-start(bf16[2,2,2,16,256]{4,3,2,1,0:T(8,128)(2,1)S(1)} %get-tuple-element.29), channel_id=1, source_target_pairs={{0,1},{1,0},{2,3},{3,2},{4,5},{5,4},{6,7},{7,6},{8,9},{9,8},{10,11... | collective-permute-start | bytes 196616 | tf_op jit(solution)/shard_map/ppermute | solution.py:470
  11.5 8.1 %collective-permute-start.1 = (bf16[2,2,2,16,256]{4,3,2,1,0:T(8,128)(2,1)S(1)}, bf16[2,2,2,16,256]{4,3,2,1,0:T(8,128)(2,1)S(1)}, u32[]{:S(2)}, u32[]{:S(2)}) collective-permute-start(bf16[2,2,2,16,256]{4,3,2,1,0:T(8,128)(2,1)S(1)} %get-tuple-element.30), channel_id=1, source_target_pairs={{0,2},{1,3},{2,0},{3,1},{4,6},{5,7},{6,4},{7,5},{8,10},{9,11},{10,... | collective-permute-start | bytes 196616 | tf_op jit(solution)/shard_map/ppermute | solution.py:470
  13.2 6.9 %collective-permute-start.2 = (bf16[2,2,2,16,256]{4,3,2,1,0:T(8,128)(2,1)S(1)}, bf16[2,2,2,16,256]{4,3,2,1,0:T(8,128)(2,1)S(1)}, u32[]{:S(2)}, u32[]{:S(2)}) collective-permute-start(bf16[2,2,2,16,256]{4,3,2,1,0:T(8,128)(2,1)S(1)} %get-tuple-element.31), channel_id=1, source_target_pairs={{0,3},{1,2},{2,1},{3,0},{4,7},{5,6},{6,5},{7,4},{8,11},{9,10},{10,... | collective-permute-start | bytes 196616 | tf_op jit(solution)/shard_map/ppermute | solution.py:470
  20.6 16.9 %collective-permute-start.3 = (bf16[4,2,16,256]{3,2,1,0:T(8,128)(2,1)S(1)}, bf16[4,2,16,256]{3,2,1,0:T(8,128)(2,1)S(1)}, u32[]{:S(2)}, u32[]{:S(2)}) collective-permute-start(bf16[4,2,16,256]{3,2,1,0:T(8,128)(2,1)S(1)} %get-tuple-element.44), channel_id=1, source_target_pairs={{0,4},{1,5},{2,6},{3,7},{4,0},{5,1},{6,2},{7,3},{8,12},{9,13},{10,... | collective-permute-start | bytes 196616 | tf_op jit(solution)/shard_map/ppermute | solution.py:515
  21.9 15.6 %collective-permute-start.4 = (bf16[4,2,16,256]{3,2,1,0:T(8,128)(2,1)S(1)}, bf16[4,2,16,256]{3,2,1,0:T(8,128)(2,1)S(1)}, u32[]{:S(2)}, u32[]{:S(2)}) collective-permute-start(bf16[4,2,16,256]{3,2,1,0:T(8,128)(2,1)S(1)} %get-tuple-element.45), channel_id=1, source_target_pairs={{0,8},{1,9},{2,10},{3,11},{4,12},{5,13},{6,14},{7,15},{8,0},{9,1},... | collective-permute-start | bytes 196616 | tf_op jit(solution)/shard_map/ppermute | solution.py:515
  25.7 11.8 %collective-permute-start.5 = (bf16[4,2,16,256]{3,2,1,0:T(8,128)(2,1)S(1)}, bf16[4,2,16,256]{3,2,1,0:T(8,128)(2,1)S(1)}, u32[]{:S(2)}, u32[]{:S(2)}) collective-permute-start(bf16[4,2,16,256]{3,2,1,0:T(8,128)(2,1)S(1)} %get-tuple-element.46), channel_id=1, source_target_pairs={{0,12},{1,13},{2,14},{3,15},{4,8},{5,9},{6,10},{7,11},{8,4},{9,5},... | collective-permute-start | bytes 196616 | tf_op jit(solution)/shard_map/ppermute | solution.py:515
  29.6 21.1 %all-to-all-start.1 = ((bf16[16,136,128]{2,1,0:T(8,128)(2,1)}), bf16[16,136,128]{2,1,0:T(8,128)(2,1)S(1)}, u32[]{:S(2)}, u32[]{:S(2)}) async-start(bf16[16,136,128]{2,1,0:T(8,128)(2,1)} %decode.1), calls=%async_computation.1 | async-start | bytes 1114112 | tf_op jit(solution)/shard_map/all_to_all | solution.py:539
